TPU v7x, 32 devices: a whole 2x2x4 slice. The times are simulated.
32 devices in a mesh: gx: 4 (over z), gy: 4 (over x, core), col: 2 (over y).
Axes of the slice: x: 2, y: 2, z: 4, core: 2. Of those that a mesh axis runs over, the one named last changes fastest.
Arguments:
- rhs: float32 [4, 4, 2, 1280, 512], P('gx', 'gy', 'col'), may hold values from -6 to 6
- stiff: bfloat16 [4, 4, 2, 1280, 2048], P('gx', 'gy', 'col'), may hold values from -0.125 to 0.125
- inv_local: bfloat16 [4, 4, 2, 1280, 2048], P('gx', 'gy', 'col'), may hold values from -0.125 to 0.125
- basis: bfloat16 [4, 4, 2, 1280, 128], P('gx', 'gy', 'col'), may hold values from -0.15625 to 0.15625
- coarse_inv: float32 [4, 2, 128, 128], P('gy', 'col'), may hold values from -0.5 to 0.5
- colors: int32 [4, 4, 2], P('gx', 'gy', 'col'), may hold values from 0 to 3
- lend: int32 [4, 4, 2, 6], P('gx', 'gy', 'col'), may hold values from 0 to 9
Outputs:
- correction: float32 [4, 4, 2, 1280, 512], P('gx', 'gy', 'col')
All inputs are finite; a program needn't handle non-finite values.
Results may differ from a plain program's by a relative error of at most 0.02.
Values may be sent and summed in bfloat16 or wider, within the bound.
A program may use at most 128 MiB of HBM per device.

v0:
```python
import jax
import jax.numpy as jnp
from jax import lax
from jax.sharding import PartitionSpec as P

BLK = 128
NCOLOR = 4


def padded(x, sides, width):
    for axis, dim in sides:
        size, length = (lax.axis_size(axis), x.shape[dim])
        up = [(i, (i + 1) % size) for i in range(size - 1)]
        down = [(j, i) for i, j in up]
        last = lax.slice_in_dim(x, length - width, length, axis=dim)
        leading = lax.slice_in_dim(x, 0, width, axis=dim)
        before = lax.ppermute(last, axis, up)
        after = lax.ppermute(leading, axis, down)
        x = jnp.concatenate([before, x, after], axis=dim)
    return x


def lent_rows(field, picks):
    return jnp.stack(
        [lax.dynamic_slice_in_dim(field, picks[which] * BLK, BLK, 0) for which in range(6)]
    )


def extend_with(field, blocks):
    wide_x = padded(blocks[0:2], (("gx", 0),), 1)
    wide_y = padded(blocks[2:4], (("gy", 0),), 1)
    wide_z = padded(blocks[4:6], (("col", 0),), 1)
    return jnp.concatenate(
        [field, wide_x[0], wide_x[3], wide_y[0], wide_y[3], wide_z[0], wide_z[3]], axis=0
    )


def body(rhs, stiff, inv_local, basis, coarse_inv, colors, lend):
    resid = rhs[0, 0, 0]
    kmat = stiff[0, 0, 0]
    ainv = inv_local[0, 0, 0]
    phi = basis[0, 0, 0]
    emat = coarse_inv[0, 0]
    color = colors[0, 0, 0]
    picks = lend[0, 0, 0]
    resid_b = resid.astype(jnp.bfloat16)
    partial_value = lax.dot_general(
        phi, resid_b, (((0,), (0,)), ((), ())), preferred_element_type=jnp.float32
    )
    coarse_rhs = lax.psum(partial_value.astype(jnp.bfloat16), "gx").astype(jnp.float32)
    coarse_sol = jnp.dot(emat, coarse_rhs, precision=lax.Precision.HIGHEST)
    coarse_b = coarse_sol.astype(jnp.bfloat16)
    coarse_delta = jnp.dot(phi, coarse_b, preferred_element_type=jnp.float32).astype(jnp.bfloat16)
    acc = coarse_delta.astype(jnp.float32)
    resid = resid - jnp.dot(
        kmat,
        extend_with(coarse_delta, lent_rows(coarse_delta, picks)),
        preferred_element_type=jnp.float32,
    )
    width = resid.shape[1]

    def solve_local(local):
        return jnp.dot(ainv, local, preferred_element_type=jnp.float32).astype(jnp.bfloat16)

    def skip_local(local):
        return jnp.zeros((ainv.shape[0], width), jnp.bfloat16)

    for color_now in range(NCOLOR):
        local_f = resid.astype(jnp.bfloat16)
        local_b = extend_with(local_f, lent_rows(local_f, picks))
        delta = lax.cond(color == color_now, solve_local, skip_local, local_b)
        acc = acc + delta.astype(jnp.float32)
        if color_now < NCOLOR - 1:
            resid = resid - jnp.dot(
                kmat,
                extend_with(delta, lent_rows(delta, picks)),
                preferred_element_type=jnp.float32,
            )
    return acc[None, None, None]


def solution(mesh):
    in_specs = (
        P("gx", "gy", "col", None, None),
        P("gx", "gy", "col", None, None),
        P("gx", "gy", "col", None, None),
        P("gx", "gy", "col", None, None),
        P("gy", "col", None, None),
        P("gx", "gy", "col"),
        P("gx", "gy", "col", None),
    )
    out_specs = P("gx", "gy", "col", None, None)
    return jax.shard_map(body, mesh=mesh, in_specs=in_specs, out_specs=out_specs, check_vma=False)
```

profile of v0, /device:TPU:0, one launch (start us, length us, event | category | flops | bytes accessed | tf_op | source)
XLA Modules:
  0.0 299.3 jit_solution(17989141810977976551)
XLA Ops:
  7.5 2.8 fusion.39
  14.9 32.7 %all-reduce.2.cloned.1.call-done = bf16[128,512]{1,0:T(8,128)(2,1)} async-done(((bf16[128,512]{1,0:T(8,128)(2,1)}), bf16[128,512]{1,0:T(8,128)(2,1)}) %all-reduce.2.cloned.1.call-update) | async-done | bytes 131088 | tf_op jit(solution)/shard_map/psum | solution.py:50
  48.8 1.6 bitcast_dynamic-update-slice_fusion
  52.4 3.3 %collective-permute-start = (bf16[1,128,512]{1,2,0:T(8,128)(2,1)}, bf16[1,128,512]{1,2,0:T(8,128)(2,1)S(1)}, u32[]{:S(2)}, u32[]{:S(2)}) collective-permute-start(bf16[1,128,512]{1,2,0:T(8,128)(2,1)} %get-tuple-element.116), channel_id=1, source_target_pairs={{0,8},{8,16},{16,24},{1,9},{9,17},{17,25},{2,10},{10,18},{18,26},{... | collective-permute-start | bytes 393224 | tf_op jit(solution)/shard_map/ppermute | solution.py:17
  55.6 2.1 copy.8
  59.0 4.6 %collective-permute-start.4 = (bf16[1,128,512]{1,2,0:T(8,128)(2,1)S(1)}, bf16[1,128,512]{1,2,0:T(8,128)(2,1)S(1)}, u32[]{:S(2)}, u32[]{:S(2)}) collective-permute-start(bf16[1,128,512]{1,2,0:T(8,128)(2,1)S(1)} %get-tuple-element.112), channel_id=1, source_target_pairs={{0,1},{2,3},{4,5},{6,7},{8,9},{10,11},{12,13},{14,15},{16,17},{18,... | collective-permute-start | bytes 393224 | tf_op jit(solution)/shard_map/ppermute | solution.py:17
  64.9 3.0 %collective-permute-start.2 = (bf16[1,128,512]{1,2,0:T(8,128)(2,1)}, bf16[1,128,512]{1,2,0:T(8,128)(2,1)S(1)}, u32[]{:S(2)}, u32[]{:S(2)}) collective-permute-start(bf16[1,128,512]{1,2,0:T(8,128)(2,1)} %get-tuple-element.114), channel_id=1, source_target_pairs={{0,2},{2,4},{4,6},{1,3},{3,5},{5,7},{8,10},{10,12},{12,14},{9,11},... | collective-permute-start | bytes 393224 | tf_op jit(solution)/shard_map/ppermute | solution.py:17
  67.9 1.3 collective-permute-start.1
  69.9 6.4 %collective-permute-done.1 = bf16[1,128,512]{1,2,0:T(8,128)(2,1)S(1)} collective-permute-done((bf16[1,128,512]{1,2,0:T(8,128)(2,1)}, bf16[1,128,512]{1,2,0:T(8,128)(2,1)S(1)}, u32[]{:S(2)}, u32[]{:S(2)}) %collective-permute-start.1) | collective-permute-done | bytes 131104 | tf_op jit(solution)/shard_map/ppermute | solution.py:18
  79.7 8.4 %constant_dynamic-update-slice_fusion = (bf16[2048,512]{0,1:T(8,128)(2,1)S(1)}, bf16[1280,512]{0,1:T(8,128)(2,1)S(1)}, f32[1280,512]{0,1:T(8,128)}) fusion(bf16[2048,512]{0,1:T(8,128)(2,1)} %bitcast_dynamic-update-slice_fusion.43, bf16[1,1,1,1280,2048]{4,3,2,1,0:T(8,128)(2,1)} %param.16, f32[1,1,1,1280,512]{3,4,2,1,0:T(8,128)} %copy.8), kind=kOutput, calls=%fused_computation.128 | convolution fusion | flops 2685665280 | bytes 15204352 | tf_op jit(solution)/shard_map/dot_general | solution.py:55
  88.3 3.2 %collective-permute-start.6 = (bf16[1,128,512]{1,2,0:T(8,128)(2,1)S(1)}, bf16[1,128,512]{1,2,0:T(8,128)(2,1)S(1)}, u32[]{:S(2)}, u32[]{:S(2)}) collective-permute-start(bf16[1,128,512]{1,2,0:T(8,128)(2,1)S(1)} %get-tuple-element.110), channel_id=1, source_target_pairs={{0,8},{8,16},{16,24},{1,9},{9,17},{17,25},{2,10},{10,18},{18,26},{... | collective-permute-start | bytes 393224 | tf_op jit(solution)/shard_map/ppermute | solution.py:17
  93.4 4.6 %collective-permute-start.10 = (bf16[1,128,512]{1,2,0:T(8,128)(2,1)S(1)}, bf16[1,128,512]{1,2,0:T(8,128)(2,1)S(1)}, u32[]{:S(2)}, u32[]{:S(2)}) collective-permute-start(bf16[1,128,512]{1,2,0:T(8,128)(2,1)S(1)} %get-tuple-element.106), channel_id=1, source_target_pairs={{0,1},{2,3},{4,5},{6,7},{8,9},{10,11},{12,13},{14,15},{16,17},{18,... | collective-permute-start | bytes 393224 | tf_op jit(solution)/shard_map/ppermute | solution.py:17
  99.3 3.0 %collective-permute-start.8 = (bf16[1,128,512]{1,2,0:T(8,128)(2,1)S(1)}, bf16[1,128,512]{1,2,0:T(8,128)(2,1)S(1)}, u32[]{:S(2)}, u32[]{:S(2)}) collective-permute-start(bf16[1,128,512]{1,2,0:T(8,128)(2,1)S(1)} %get-tuple-element.108), channel_id=1, source_target_pairs={{0,2},{2,4},{4,6},{1,3},{3,5},{5,7},{8,10},{10,12},{12,14},{9,11},... | collective-permute-start | bytes 393224 | tf_op jit(solution)/shard_map/ppermute | solution.py:17
  103.7 6.5 %collective-permute-done.7 = bf16[1,128,512]{1,2,0:T(8,128)(2,1)S(1)} collective-permute-done((bf16[1,128,512]{1,2,0:T(8,128)(2,1)S(1)}, bf16[1,128,512]{1,2,0:T(8,128)(2,1)S(1)}, u32[]{:S(2)}, u32[]{:S(2)}) %collective-permute-start.7) | collective-permute-done | bytes 131104 | tf_op jit(solution)/shard_map/ppermute | solution.py:18
  110.4 1.3 conditional.4
  111.8 2.1 dynamic-slice_bitcast_fusion.30
  113.9 2.8 collective-permute-start.12
  116.7 1.4 constant_dynamic-update-slice_fusion.1
  119.4 4.6 %collective-permute-start.16 = (bf16[1,128,512]{2,1,0:T(8,128)(2,1)S(1)}, bf16[1,128,512]{2,1,0:T(8,128)(2,1)S(1)}, u32[]{:S(2)}, u32[]{:S(2)}) collective-permute-start(bf16[1,128,512]{2,1,0:T(8,128)(2,1)S(1)} %get-tuple-element.100), channel_id=1, source_target_pairs={{0,1},{2,3},{4,5},{6,7},{8,9},{10,11},{12,13},{14,15},{16,17},{18,... | collective-permute-start | bytes 393224 | tf_op jit(solution)/shard_map/ppermute | solution.py:17
  125.3 3.0 %collective-permute-start.14 = (bf16[1,128,512]{2,1,0:T(8,128)(2,1)S(1)}, bf16[1,128,512]{2,1,0:T(8,128)(2,1)S(1)}, u32[]{:S(2)}, u32[]{:S(2)}) collective-permute-start(bf16[1,128,512]{2,1,0:T(8,128)(2,1)S(1)} %get-tuple-element.102), channel_id=1, source_target_pairs={{0,2},{2,4},{4,6},{1,3},{3,5},{5,7},{8,10},{10,12},{12,14},{9,11},... | collective-permute-start | bytes 393224 | tf_op jit(solution)/shard_map/ppermute | solution.py:17
  128.3 1.5 collective-permute-start.13
  129.8 8.7 %collective-permute-done.13 = bf16[1,128,512]{2,1,0:T(8,128)(2,1)S(1)} collective-permute-done((bf16[1,128,512]{2,1,0:T(8,128)(2,1)S(1)}, bf16[1,128,512]{2,1,0:T(8,128)(2,1)S(1)}, u32[]{:S(2)}, u32[]{:S(2)}) %collective-permute-start.13) | collective-permute-done | bytes 131104 | tf_op jit(solution)/shard_map/ppermute | solution.py:18
  138.7 7.1 %constant_dynamic-update-slice_fusion.2 = (bf16[2048,512]{0,1:T(8,128)(2,1)S(1)}, bf16[1280,512]{0,1:T(8,128)(2,1)S(1)}, f32[1280,512]{0,1:T(8,128)}) fusion(f32[1280,512]{0,1:T(8,128)S(1)} %copy-done.10, bf16[2048,512]{1,0:T(8,128)(2,1)S(1)} %bitcast_dynamic-update-slice_fusion.31, bf16[1,1,1,1280,2048]{4,3,2,1,0:T(8,128)(2,1)} %param.16), kind=kOutput, calls=%fused_computation.130 | convolution fusion | flops 2685665280 | bytes 15204352 | tf_op jit(solution)/shard_map/dot_general | solution.py:74
  145.9 3.6 %collective-permute-start.18 = (bf16[1,128,512]{1,2,0:T(8,128)(2,1)S(1)}, bf16[1,128,512]{1,2,0:T(8,128)(2,1)S(1)}, u32[]{:S(2)}, u32[]{:S(2)}) collective-permute-start(bf16[1,128,512]{1,2,0:T(8,128)(2,1)S(1)} %get-tuple-element.98), channel_id=1, source_target_pairs={{0,8},{8,16},{16,24},{1,9},{9,17},{17,25},{2,10},{10,18},{18,26},{... | collective-permute-start | bytes 393224 | tf_op jit(solution)/shard_map/ppermute | solution.py:17
  150.9 4.6 %collective-permute-start.22 = (bf16[1,128,512]{1,2,0:T(8,128)(2,1)S(1)}, bf16[1,128,512]{1,2,0:T(8,128)(2,1)S(1)}, u32[]{:S(2)}, u32[]{:S(2)}) collective-permute-start(bf16[1,128,512]{1,2,0:T(8,128)(2,1)S(1)} %get-tuple-element.94), channel_id=1, source_target_pairs={{0,1},{2,3},{4,5},{6,7},{8,9},{10,11},{12,13},{14,15},{16,17},{18,... | collective-permute-start | bytes 393224 | tf_op jit(solution)/shard_map/ppermute | solution.py:17
  155.5 1.3 collective-permute-start.21
  156.8 3.0 %collective-permute-start.20 = (bf16[1,128,512]{1,2,0:T(8,128)(2,1)S(1)}, bf16[1,128,512]{1,2,0:T(8,128)(2,1)S(1)}, u32[]{:S(2)}, u32[]{:S(2)}) collective-permute-start(bf16[1,128,512]{1,2,0:T(8,128)(2,1)S(1)} %get-tuple-element.96), channel_id=1, source_target_pairs={{0,2},{2,4},{4,6},{1,3},{3,5},{5,7},{8,10},{10,12},{12,14},{9,11},... | collective-permute-start | bytes 393224 | tf_op jit(solution)/shard_map/ppermute | solution.py:17
  161.2 6.0 %collective-permute-done.19 = bf16[1,128,512]{1,2,0:T(8,128)(2,1)S(1)} collective-permute-done((bf16[1,128,512]{1,2,0:T(8,128)(2,1)S(1)}, bf16[1,128,512]{1,2,0:T(8,128)(2,1)S(1)}, u32[]{:S(2)}, u32[]{:S(2)}) %collective-permute-start.19) | collective-permute-done | bytes 131104 | tf_op jit(solution)/shard_map/ppermute | solution.py:18
  167.4 1.4 conditional.5
  168.8 2.1 dynamic-slice_bitcast_fusion.18
  170.9 6.5 %collective-permute-start.24 = (bf16[1,128,512]{2,1,0:T(8,128)(2,1)S(1)}, bf16[1,128,512]{2,1,0:T(8,128)(2,1)S(1)}, u32[]{:S(2)}, u32[]{:S(2)}) collective-permute-start(bf16[1,128,512]{2,1,0:T(8,128)(2,1)S(1)} %get-tuple-element.92), channel_id=1, source_target_pairs={{0,8},{8,16},{16,24},{1,9},{9,17},{17,25},{2,10},{10,18},{18,26},{... | collective-permute-start | bytes 393224 | tf_op jit(solution)/shard_map/ppermute | solution.py:17
  177.4 1.4 constant_dynamic-update-slice_fusion.3
  178.8 1.3 collective-permute-start.29
  180.1 4.6 %collective-permute-start.28 = (bf16[1,128,512]{2,1,0:T(8,128)(2,1)S(1)}, bf16[1,128,512]{2,1,0:T(8,128)(2,1)S(1)}, u32[]{:S(2)}, u32[]{:S(2)}) collective-permute-start(bf16[1,128,512]{2,1,0:T(8,128)(2,1)S(1)} %get-tuple-element.88), channel_id=1, source_target_pairs={{0,1},{2,3},{4,5},{6,7},{8,9},{10,11},{12,13},{14,15},{16,17},{18,... | collective-permute-start | bytes 393224 | tf_op jit(solution)/shard_map/ppermute | solution.py:17
  184.7 1.3 collective-permute-start.27
  186.0 3.0 %collective-permute-start.26 = (bf16[1,128,512]{2,1,0:T(8,128)(2,1)S(1)}, bf16[1,128,512]{2,1,0:T(8,128)(2,1)S(1)}, u32[]{:S(2)}, u32[]{:S(2)}) collective-permute-start(bf16[1,128,512]{2,1,0:T(8,128)(2,1)S(1)} %get-tuple-element.90), channel_id=1, source_target_pairs={{0,2},{2,4},{4,6},{1,3},{3,5},{5,7},{8,10},{10,12},{12,14},{9,11},... | collective-permute-start | bytes 393224 | tf_op jit(solution)/shard_map/ppermute | solution.py:17
  190.4 6.0 %collective-permute-done.25 = bf16[1,128,512]{2,1,0:T(8,128)(2,1)S(1)} collective-permute-done((bf16[1,128,512]{2,1,0:T(8,128)(2,1)S(1)}, bf16[1,128,512]{2,1,0:T(8,128)(2,1)S(1)}, u32[]{:S(2)}, u32[]{:S(2)}) %collective-permute-start.25) | collective-permute-done | bytes 131104 | tf_op jit(solution)/shard_map/ppermute | solution.py:18
  196.5 7.1 %constant_dynamic-update-slice_fusion.4 = (bf16[2048,512]{0,1:T(8,128)(2,1)S(1)}, bf16[1280,512]{0,1:T(8,128)(2,1)S(1)}, f32[1280,512]{0,1:T(8,128)}) fusion(f32[1280,512]{0,1:T(8,128)S(1)} %copy-done.11, bf16[2048,512]{1,0:T(8,128)(2,1)S(1)} %bitcast_dynamic-update-slice_fusion.19, bf16[1,1,1,1280,2048]{4,3,2,1,0:T(8,128)(2,1)} %param.16), kind=kOutput, calls=%fused_computation.132 | convolution fusion | flops 2685665280 | bytes 15204352 | tf_op jit(solution)/shard_map/dot_general | solution.py:74
  203.7 1.9 collective-permute-start.30
  205.6 1.3 collective-permute-start.35
  206.9 4.6 %collective-permute-start.34 = (bf16[1,128,512]{1,2,0:T(8,128)(2,1)S(1)}, bf16[1,128,512]{1,2,0:T(8,128)(2,1)S(1)}, u32[]{:S(2)}, u32[]{:S(2)}) collective-permute-start(bf16[1,128,512]{1,2,0:T(8,128)(2,1)S(1)} %get-tuple-element.82), channel_id=1, source_target_pairs={{0,1},{2,3},{4,5},{6,7},{8,9},{10,11},{12,13},{14,15},{16,17},{18,... | collective-permute-start | bytes 393224 | tf_op jit(solution)/shard_map/ppermute | solution.py:17
  211.5 1.3 collective-permute-start.33
  212.8 3.0 %collective-permute-start.32 = (bf16[1,128,512]{1,2,0:T(8,128)(2,1)S(1)}, bf16[1,128,512]{1,2,0:T(8,128)(2,1)S(1)}, u32[]{:S(2)}, u32[]{:S(2)}) collective-permute-start(bf16[1,128,512]{1,2,0:T(8,128)(2,1)S(1)} %get-tuple-element.84), channel_id=1, source_target_pairs={{0,2},{2,4},{4,6},{1,3},{3,5},{5,7},{8,10},{10,12},{12,14},{9,11},... | collective-permute-start | bytes 393224 | tf_op jit(solution)/shard_map/ppermute | solution.py:17
  217.2 6.0 %collective-permute-done.31 = bf16[1,128,512]{1,2,0:T(8,128)(2,1)S(1)} collective-permute-done((bf16[1,128,512]{1,2,0:T(8,128)(2,1)S(1)}, bf16[1,128,512]{1,2,0:T(8,128)(2,1)S(1)}, u32[]{:S(2)}, u32[]{:S(2)}) %collective-permute-start.31) | collective-permute-done | bytes 131104 | tf_op jit(solution)/shard_map/ppermute | solution.py:18
  223.5 1.6 conditional.6
  225.0 2.1 dynamic-slice_bitcast_fusion.6
  227.1 2.2 collective-permute-start.36
  229.3 1.6 constant_dynamic-update-slice_fusion.5
  230.9 1.4 collective-permute-start.41
  232.3 4.6 %collective-permute-start.40 = (bf16[1,128,512]{2,1,0:T(8,128)(2,1)S(1)}, bf16[1,128,512]{2,1,0:T(8,128)(2,1)S(1)}, u32[]{:S(2)}, u32[]{:S(2)}) collective-permute-start(bf16[1,128,512]{2,1,0:T(8,128)(2,1)S(1)} %get-tuple-element.76), channel_id=1, source_target_pairs={{0,1},{2,3},{4,5},{6,7},{8,9},{10,11},{12,13},{14,15},{16,17},{18,... | collective-permute-start | bytes 393224 | tf_op jit(solution)/shard_map/ppermute | solution.py:17
  236.9 1.3 collective-permute-start.39
  238.2 3.0 %collective-permute-start.38 = (bf16[1,128,512]{2,1,0:T(8,128)(2,1)S(1)}, bf16[1,128,512]{2,1,0:T(8,128)(2,1)S(1)}, u32[]{:S(2)}, u32[]{:S(2)}) collective-permute-start(bf16[1,128,512]{2,1,0:T(8,128)(2,1)S(1)} %get-tuple-element.78), channel_id=1, source_target_pairs={{0,2},{2,4},{4,6},{1,3},{3,5},{5,7},{8,10},{10,12},{12,14},{9,11},... | collective-permute-start | bytes 393224 | tf_op jit(solution)/shard_map/ppermute | solution.py:17
  242.6 6.3 %collective-permute-done.37 = bf16[1,128,512]{2,1,0:T(8,128)(2,1)S(1)} collective-permute-done((bf16[1,128,512]{2,1,0:T(8,128)(2,1)S(1)}, bf16[1,128,512]{2,1,0:T(8,128)(2,1)S(1)}, u32[]{:S(2)}, u32[]{:S(2)}) %collective-permute-start.37) | collective-permute-done | bytes 131104 | tf_op jit(solution)/shard_map/ppermute | solution.py:18
  249.0 5.6 %constant_dynamic-update-slice_fusion.6 = (bf16[2048,512]{0,1:T(8,128)(2,1)S(1)}, bf16[1280,512]{0,1:T(8,128)(2,1)S(1)}) fusion(f32[1280,512]{0,1:T(8,128)S(1)} %copy-done.12, bf16[2048,512]{1,0:T(8,128)(2,1)S(1)} %bitcast_dynamic-update-slice_fusion.7, bf16[1,1,1,1280,2048]{4,3,2,1,0:T(8,128)(2,1)} %param.16), kind=kOutput, calls=%fused_computation.134 | convolution fusion | flops 2685665280 | bytes 12582912 | tf_op jit(solution)/shard_map/dot_general | solution.py:74
  254.8 3.5 %collective-permute-start.42 = (bf16[1,128,512]{1,2,0:T(8,128)(2,1)S(1)}, bf16[1,128,512]{1,2,0:T(8,128)(2,1)S(1)}, u32[]{:S(2)}, u32[]{:S(2)}) collective-permute-start(bf16[1,128,512]{1,2,0:T(8,128)(2,1)S(1)} %get-tuple-element.74), channel_id=1, source_target_pairs={{0,8},{8,16},{16,24},{1,9},{9,17},{17,25},{2,10},{10,18},{18,26},{... | collective-permute-start | bytes 393224 | tf_op jit(solution)/shard_map/ppermute | solution.py:17
  259.6 4.6 %collective-permute-start.46 = (bf16[1,128,512]{1,2,0:T(8,128)(2,1)S(1)}, bf16[1,128,512]{1,2,0:T(8,128)(2,1)S(1)}, u32[]{:S(2)}, u32[]{:S(2)}) collective-permute-start(bf16[1,128,512]{1,2,0:T(8,128)(2,1)S(1)} %get-tuple-element.70), channel_id=1, source_target_pairs={{0,1},{2,3},{4,5},{6,7},{8,9},{10,11},{12,13},{14,15},{16,17},{18,... | collective-permute-start | bytes 393224 | tf_op jit(solution)/shard_map/ppermute | solution.py:17
  265.5 3.0 %collective-permute-start.44 = (bf16[1,128,512]{1,2,0:T(8,128)(2,1)S(1)}, bf16[1,128,512]{1,2,0:T(8,128)(2,1)S(1)}, u32[]{:S(2)}, u32[]{:S(2)}) collective-permute-start(bf16[1,128,512]{1,2,0:T(8,128)(2,1)S(1)} %get-tuple-element.72), channel_id=1, source_target_pairs={{0,2},{2,4},{4,6},{1,3},{3,5},{5,7},{8,10},{10,12},{12,14},{9,11},... | collective-permute-start | bytes 393224 | tf_op jit(solution)/shard_map/ppermute | solution.py:17
  269.9 6.9 %collective-permute-done.43 = bf16[1,128,512]{1,2,0:T(8,128)(2,1)S(1)} collective-permute-done((bf16[1,128,512]{1,2,0:T(8,128)(2,1)S(1)}, bf16[1,128,512]{1,2,0:T(8,128)(2,1)S(1)}, u32[]{:S(2)}, u32[]{:S(2)}) %collective-permute-start.43) | collective-permute-done | bytes 131104 | tf_op jit(solution)/shard_map/ppermute | solution.py:18
  277.1 6.6 %conditional.7 = (f32[1280,512]{0,1:T(8,128)S(1)}) conditional(s32[]{:T(128)} %bitcast.97, () %tuple.49, (bf16[1280,2048]{1,0:T(8,128)(2,1)S(1)}, bf16[2048,512]{0,1:T(8,128)(2,1)S(1)}) %tuple.129), branch_computations={%region_7.0_spmd, %region_8.0_spmd} | conditional | flops 2685665280 | bytes 15204360 | solution.py:71
  277.1 4.5 %fusion = f32[1280,512]{1,0:T(8,128)} fusion(bf16[1280,2048]{1,0:T(8,128)(2,1)S(1)} %get-tuple-element.37, bf16[2048,512]{0,1:T(8,128)(2,1)S(1)} %get-tuple-element.58), kind=kOutput, calls=%fused_computation.4 | convolution fusion | flops 2685665280 | bytes 9961472 | tf_op jit(solution)/shard_map/cond/branch_1_fun/dot_general | solution.py:63
  281.6 2.1 copy.29
  283.7 1.5 copy-done.5
  285.2 5.1 %add_bitcast_fusion = f32[1,1,1,1280,512]{3,4,2,1,0:T(8,128)S(1)} fusion(f32[1280,512]{0,1:T(8,128)} %copy-done.5, f32[1280,512]{0,1:T(8,128)} %copy-done.4, f32[1280,512]{0,1:T(8,128)} %copy-done.3, f32[1280,512]{0,1:T(8,128)} %copy-done.2, bf16[512,1280]{1,0:T(8,128)(2,1)} %copy-done.7), kind=kLoop, calls=%fused_computation.23 | loop fusion | flops 3276800 | bytes 14417920 | tf_op jit(solution)/shard_map/broadcast_in_dim | solution.py:79
  290.4 2.1 copy.17
  (163 shorter events, 34.2 us)
Async XLA Ops:
  6.5 41.1 %copy-start.8 = (f32[1,1,128,128]{3,2,1,0:T(8,128)S(1)}, f32[1,1,128,128]{3,2,1,0:T(8,128)}, u32[]{:S(2)}) copy-start(f32[1,1,128,128]{3,2,1,0:T(8,128)} %param.19) | copy-start | bytes 196612
  6.5 41.1 %all-reduce.2.cloned.1.call-start = ((), (), s32[]{:S(2)}) async-start(), calls=%async_computation | async-start | bytes 262144 | tf_op jit(solution)/shard_map/psum | solution.py:50
  48.8 6.8 %copy-start.6 = (f32[1,1,1,1280,512]{4,3,2,1,0:T(8,128)S(1)}, f32[1,1,1,1280,512]{4,3,2,1,0:T(8,128)}, u32[]{:S(2)}) copy-start(f32[1,1,1,1280,512]{4,3,2,1,0:T(8,128)} %param.15) | copy-start | bytes 7864324
  52.4 15.6 %collective-permute-start = (bf16[1,128,512]{1,2,0:T(8,128)(2,1)}, bf16[1,128,512]{1,2,0:T(8,128)(2,1)S(1)}, u32[]{:S(2)}, u32[]{:S(2)}) collective-permute-start(bf16[1,128,512]{1,2,0:T(8,128)(2,1)} %get-tuple-element.116), channel_id=1, source_target_pairs={{0,8},{8,16},{16,24},{1,9},{9,17},{17,25},{2,10},{10,18},{18,26},{... | collective-permute-start | bytes 393224 | tf_op jit(solution)/shard_map/ppermute | solution.py:17
  57.7 21.3 %collective-permute-start.5 = (bf16[1,128,512]{1,2,0:T(8,128)(2,1)S(1)}, bf16[1,128,512]{1,2,0:T(8,128)(2,1)S(1)}, u32[]{:S(2)}, u32[]{:S(2)}) collective-permute-start(bf16[1,128,512]{1,2,0:T(8,128)(2,1)S(1)} %get-tuple-element.111), channel_id=1, source_target_pairs={{1,0},{3,2},{5,4},{7,6},{9,8},{11,10},{13,12},{15,14},{17,16},{19,... | collective-permute-start | bytes 393224 | tf_op jit(solution)/shard_map/ppermute | solution.py:18
  59.0 19.4 %collective-permute-start.4 = (bf16[1,128,512]{1,2,0:T(8,128)(2,1)S(1)}, bf16[1,128,512]{1,2,0:T(8,128)(2,1)S(1)}, u32[]{:S(2)}, u32[]{:S(2)}) collective-permute-start(bf16[1,128,512]{1,2,0:T(8,128)(2,1)S(1)} %get-tuple-element.112), channel_id=1, source_target_pairs={{0,1},{2,3},{4,5},{6,7},{8,9},{10,11},{12,13},{14,15},{16,17},{18,... | collective-permute-start | bytes 393224 | tf_op jit(solution)/shard_map/ppermute | solution.py:17
  63.6 14.1 %collective-permute-start.3 = (bf16[1,128,512]{1,2,0:T(8,128)(2,1)S(1)}, bf16[1,128,512]{1,2,0:T(8,128)(2,1)S(1)}, u32[]{:S(2)}, u32[]{:S(2)}) collective-permute-start(bf16[1,128,512]{1,2,0:T(8,128)(2,1)S(1)} %get-tuple-element.113), channel_id=1, source_target_pairs={{2,0},{4,2},{6,4},{3,1},{5,3},{7,5},{10,8},{12,10},{14,12},{11,9},... | collective-permute-start | bytes 393224 | tf_op jit(solution)/shard_map/ppermute | solution.py:18
  64.9 12.1 %collective-permute-start.2 = (bf16[1,128,512]{1,2,0:T(8,128)(2,1)}, bf16[1,128,512]{1,2,0:T(8,128)(2,1)S(1)}, u32[]{:S(2)}, u32[]{:S(2)}) collective-permute-start(bf16[1,128,512]{1,2,0:T(8,128)(2,1)} %get-tuple-element.114), channel_id=1, source_target_pairs={{0,2},{2,4},{4,6},{1,3},{3,5},{5,7},{8,10},{10,12},{12,14},{9,11},... | collective-permute-start | bytes 393224 | tf_op jit(solution)/shard_map/ppermute | solution.py:17
  67.9 8.4 %collective-permute-start.1 = (bf16[1,128,512]{1,2,0:T(8,128)(2,1)}, bf16[1,128,512]{1,2,0:T(8,128)(2,1)S(1)}, u32[]{:S(2)}, u32[]{:S(2)}) collective-permute-start(bf16[1,128,512]{1,2,0:T(8,128)(2,1)} %get-tuple-element.115), channel_id=1, source_target_pairs={{8,0},{16,8},{24,16},{9,1},{17,9},{25,17},{10,2},{18,10},{26,18},{... | collective-permute-start | bytes 393224 | tf_op jit(solution)/shard_map/ppermute | solution.py:18
  78.4 32.0 %slice-start = ((s8[5242880]{0:T(1024)(128)(4,1)}), s8[4194304]{0:T(1024)(128)(4,1)S(1)}, s32[]{:S(2)}) async-start(s8[5242880]{0:T(1024)(128)(4,1)} %bitcast.304), calls=%async_computation.1 | async-start | bytes 8388608
  79.7 30.7 %slice-start.1 = ((s8[5242880]{0:T(1024)(128)(4,1)}), s8[1048576]{0:T(1024)(128)(4,1)S(1)}, s32[]{:S(2)}) async-start(s8[5242880]{0:T(1024)(128)(4,1)} %bitcast.304), calls=%async_computation.2 | async-start | bytes 2097152
  88.3 14.0 %collective-permute-start.6 = (bf16[1,128,512]{1,2,0:T(8,128)(2,1)S(1)}, bf16[1,128,512]{1,2,0:T(8,128)(2,1)S(1)}, u32[]{:S(2)}, u32[]{:S(2)}) collective-permute-start(bf16[1,128,512]{1,2,0:T(8,128)(2,1)S(1)} %get-tuple-element.110), channel_id=1, source_target_pairs={{0,8},{8,16},{16,24},{1,9},{9,17},{17,25},{2,10},{10,18},{18,26},{... | collective-permute-start | bytes 393224 | tf_op jit(solution)/shard_map/ppermute | solution.py:17
  92.1 18.3 %collective-permute-start.11 = (bf16[1,128,512]{1,2,0:T(8,128)(2,1)S(1)}, bf16[1,128,512]{1,2,0:T(8,128)(2,1)S(1)}, u32[]{:S(2)}, u32[]{:S(2)}) collective-permute-start(bf16[1,128,512]{1,2,0:T(8,128)(2,1)S(1)} %get-tuple-element.105), channel_id=1, source_target_pairs={{1,0},{3,2},{5,4},{7,6},{9,8},{11,10},{13,12},{15,14},{17,16},{19,... | collective-permute-start | bytes 393224 | tf_op jit(solution)/shard_map/ppermute | solution.py:18
  93.4 16.9 %collective-permute-start.10 = (bf16[1,128,512]{1,2,0:T(8,128)(2,1)S(1)}, bf16[1,128,512]{1,2,0:T(8,128)(2,1)S(1)}, u32[]{:S(2)}, u32[]{:S(2)}) collective-permute-start(bf16[1,128,512]{1,2,0:T(8,128)(2,1)S(1)} %get-tuple-element.106), channel_id=1, source_target_pairs={{0,1},{2,3},{4,5},{6,7},{8,9},{10,11},{12,13},{14,15},{16,17},{18,... | collective-permute-start | bytes 393224 | tf_op jit(solution)/shard_map/ppermute | solution.py:17
  98.0 12.3 %collective-permute-start.9 = (bf16[1,128,512]{1,2,0:T(8,128)(2,1)S(1)}, bf16[1,128,512]{1,2,0:T(8,128)(2,1)S(1)}, u32[]{:S(2)}, u32[]{:S(2)}) collective-permute-start(bf16[1,128,512]{1,2,0:T(8,128)(2,1)S(1)} %get-tuple-element.107), channel_id=1, source_target_pairs={{2,0},{4,2},{6,4},{3,1},{5,3},{7,5},{10,8},{12,10},{14,12},{11,9},... | collective-permute-start | bytes 393224 | tf_op jit(solution)/shard_map/ppermute | solution.py:18
  99.3 10.9 %collective-permute-start.8 = (bf16[1,128,512]{1,2,0:T(8,128)(2,1)S(1)}, bf16[1,128,512]{1,2,0:T(8,128)(2,1)S(1)}, u32[]{:S(2)}, u32[]{:S(2)}) collective-permute-start(bf16[1,128,512]{1,2,0:T(8,128)(2,1)S(1)} %get-tuple-element.108), channel_id=1, source_target_pairs={{0,2},{2,4},{4,6},{1,3},{3,5},{5,7},{8,10},{10,12},{12,14},{9,11},... | collective-permute-start | bytes 393224 | tf_op jit(solution)/shard_map/ppermute | solution.py:17
  102.3 7.8 %collective-permute-start.7 = (bf16[1,128,512]{1,2,0:T(8,128)(2,1)S(1)}, bf16[1,128,512]{1,2,0:T(8,128)(2,1)S(1)}, u32[]{:S(2)}, u32[]{:S(2)}) collective-permute-start(bf16[1,128,512]{1,2,0:T(8,128)(2,1)S(1)} %get-tuple-element.109), channel_id=1, source_target_pairs={{8,0},{16,8},{24,16},{9,1},{17,9},{25,17},{10,2},{18,10},{26,18},{... | collective-permute-start | bytes 393224 | tf_op jit(solution)/shard_map/ppermute | solution.py:18
  113.9 24.8 %copy-start.10 = (f32[1280,512]{0,1:T(8,128)S(1)}, f32[1280,512]{0,1:T(8,128)}, u32[]{:S(2)}) copy-start(f32[1280,512]{0,1:T(8,128)} %get-tuple-element.125) | copy-start | bytes 7864324
  113.9 14.4 %collective-permute-start.12 = (bf16[1,128,512]{2,1,0:T(8,128)(2,1)S(1)}, bf16[1,128,512]{2,1,0:T(8,128)(2,1)S(1)}, u32[]{:S(2)}, u32[]{:S(2)}) collective-permute-start(bf16[1,128,512]{2,1,0:T(8,128)(2,1)S(1)} %get-tuple-element.104), channel_id=1, source_target_pairs={{0,8},{8,16},{16,24},{1,9},{9,17},{17,25},{2,10},{10,18},{18,26},{... | collective-permute-start | bytes 393224 | tf_op jit(solution)/shard_map/ppermute | solution.py:17
  118.1 20.5 %collective-permute-start.17 = (bf16[1,128,512]{2,1,0:T(8,128)(2,1)S(1)}, bf16[1,128,512]{2,1,0:T(8,128)(2,1)S(1)}, u32[]{:S(2)}, u32[]{:S(2)}) collective-permute-start(bf16[1,128,512]{2,1,0:T(8,128)(2,1)S(1)} %get-tuple-element.99), channel_id=1, source_target_pairs={{1,0},{3,2},{5,4},{7,6},{9,8},{11,10},{13,12},{15,14},{17,16},{19,... | collective-permute-start | bytes 393224 | tf_op jit(solution)/shard_map/ppermute | solution.py:18
  119.4 19.2 %collective-permute-start.16 = (bf16[1,128,512]{2,1,0:T(8,128)(2,1)S(1)}, bf16[1,128,512]{2,1,0:T(8,128)(2,1)S(1)}, u32[]{:S(2)}, u32[]{:S(2)}) collective-permute-start(bf16[1,128,512]{2,1,0:T(8,128)(2,1)S(1)} %get-tuple-element.100), channel_id=1, source_target_pairs={{0,1},{2,3},{4,5},{6,7},{8,9},{10,11},{12,13},{14,15},{16,17},{18,... | collective-permute-start | bytes 393224 | tf_op jit(solution)/shard_map/ppermute | solution.py:17
  124.0 14.6 %collective-permute-start.15 = (bf16[1,128,512]{2,1,0:T(8,128)(2,1)S(1)}, bf16[1,128,512]{2,1,0:T(8,128)(2,1)S(1)}, u32[]{:S(2)}, u32[]{:S(2)}) collective-permute-start(bf16[1,128,512]{2,1,0:T(8,128)(2,1)S(1)} %get-tuple-element.101), channel_id=1, source_target_pairs={{2,0},{4,2},{6,4},{3,1},{5,3},{7,5},{10,8},{12,10},{14,12},{11,9},... | collective-permute-start | bytes 393224 | tf_op jit(solution)/shard_map/ppermute | solution.py:18
  125.3 13.2 %collective-permute-start.14 = (bf16[1,128,512]{2,1,0:T(8,128)(2,1)S(1)}, bf16[1,128,512]{2,1,0:T(8,128)(2,1)S(1)}, u32[]{:S(2)}, u32[]{:S(2)}) collective-permute-start(bf16[1,128,512]{2,1,0:T(8,128)(2,1)S(1)} %get-tuple-element.102), channel_id=1, source_target_pairs={{0,2},{2,4},{4,6},{1,3},{3,5},{5,7},{8,10},{10,12},{12,14},{9,11},... | collective-permute-start | bytes 393224 | tf_op jit(solution)/shard_map/ppermute | solution.py:17
  128.3 10.2 %collective-permute-start.13 = (bf16[1,128,512]{2,1,0:T(8,128)(2,1)S(1)}, bf16[1,128,512]{2,1,0:T(8,128)(2,1)S(1)}, u32[]{:S(2)}, u32[]{:S(2)}) collective-permute-start(bf16[1,128,512]{2,1,0:T(8,128)(2,1)S(1)} %get-tuple-element.103), channel_id=1, source_target_pairs={{8,0},{16,8},{24,16},{9,1},{17,9},{25,17},{10,2},{18,10},{26,18},{... | collective-permute-start | bytes 393224 | tf_op jit(solution)/shard_map/ppermute | solution.py:18
  138.5 28.9 %slice-start.2 = ((s8[5242880]{0:T(1024)(128)(4,1)}), s8[4194304]{0:T(1024)(128)(4,1)S(1)}, s32[]{:S(2)}) async-start(s8[5242880]{0:T(1024)(128)(4,1)} %bitcast.307), calls=%async_computation.3 | async-start | bytes 8388608
  138.6 28.8 %slice-start.3 = ((s8[5242880]{0:T(1024)(128)(4,1)}), s8[1048576]{0:T(1024)(128)(4,1)S(1)}, s32[]{:S(2)}) async-start(s8[5242880]{0:T(1024)(128)(4,1)} %bitcast.307), calls=%async_computation.4 | async-start | bytes 2097152
  145.9 13.9 %collective-permute-start.18 = (bf16[1,128,512]{1,2,0:T(8,128)(2,1)S(1)}, bf16[1,128,512]{1,2,0:T(8,128)(2,1)S(1)}, u32[]{:S(2)}, u32[]{:S(2)}) collective-permute-start(bf16[1,128,512]{1,2,0:T(8,128)(2,1)S(1)} %get-tuple-element.98), channel_id=1, source_target_pairs={{0,8},{8,16},{16,24},{1,9},{9,17},{17,25},{2,10},{10,18},{18,26},{... | collective-permute-start | bytes 393224 | tf_op jit(solution)/shard_map/ppermute | solution.py:17
  149.6 17.7 %collective-permute-start.23 = (bf16[1,128,512]{1,2,0:T(8,128)(2,1)S(1)}, bf16[1,128,512]{1,2,0:T(8,128)(2,1)S(1)}, u32[]{:S(2)}, u32[]{:S(2)}) collective-permute-start(bf16[1,128,512]{1,2,0:T(8,128)(2,1)S(1)} %get-tuple-element.93), channel_id=1, source_target_pairs={{1,0},{3,2},{5,4},{7,6},{9,8},{11,10},{13,12},{15,14},{17,16},{19,... | collective-permute-start | bytes 393224 | tf_op jit(solution)/shard_map/ppermute | solution.py:18
  150.9 16.4 %collective-permute-start.22 = (bf16[1,128,512]{1,2,0:T(8,128)(2,1)S(1)}, bf16[1,128,512]{1,2,0:T(8,128)(2,1)S(1)}, u32[]{:S(2)}, u32[]{:S(2)}) collective-permute-start(bf16[1,128,512]{1,2,0:T(8,128)(2,1)S(1)} %get-tuple-element.94), channel_id=1, source_target_pairs={{0,1},{2,3},{4,5},{6,7},{8,9},{10,11},{12,13},{14,15},{16,17},{18,... | collective-permute-start | bytes 393224 | tf_op jit(solution)/shard_map/ppermute | solution.py:17
  155.5 11.8 %collective-permute-start.21 = (bf16[1,128,512]{1,2,0:T(8,128)(2,1)S(1)}, bf16[1,128,512]{1,2,0:T(8,128)(2,1)S(1)}, u32[]{:S(2)}, u32[]{:S(2)}) collective-permute-start(bf16[1,128,512]{1,2,0:T(8,128)(2,1)S(1)} %get-tuple-element.95), channel_id=1, source_target_pairs={{2,0},{4,2},{6,4},{3,1},{5,3},{7,5},{10,8},{12,10},{14,12},{11,9},... | collective-permute-start | bytes 393224 | tf_op jit(solution)/shard_map/ppermute | solution.py:18
  156.8 10.4 %collective-permute-start.20 = (bf16[1,128,512]{1,2,0:T(8,128)(2,1)S(1)}, bf16[1,128,512]{1,2,0:T(8,128)(2,1)S(1)}, u32[]{:S(2)}, u32[]{:S(2)}) collective-permute-start(bf16[1,128,512]{1,2,0:T(8,128)(2,1)S(1)} %get-tuple-element.96), channel_id=1, source_target_pairs={{0,2},{2,4},{4,6},{1,3},{3,5},{5,7},{8,10},{10,12},{12,14},{9,11},... | collective-permute-start | bytes 393224 | tf_op jit(solution)/shard_map/ppermute | solution.py:17
  159.8 7.3 %collective-permute-start.19 = (bf16[1,128,512]{1,2,0:T(8,128)(2,1)S(1)}, bf16[1,128,512]{1,2,0:T(8,128)(2,1)S(1)}, u32[]{:S(2)}, u32[]{:S(2)}) collective-permute-start(bf16[1,128,512]{1,2,0:T(8,128)(2,1)S(1)} %get-tuple-element.97), channel_id=1, source_target_pairs={{8,0},{16,8},{24,16},{9,1},{17,9},{25,17},{10,2},{18,10},{26,18},{... | collective-permute-start | bytes 393224 | tf_op jit(solution)/shard_map/ppermute | solution.py:18
  168.8 10.0 %copy-start.3 = (f32[1280,512]{0,1:T(8,128)}, f32[1280,512]{0,1:T(8,128)S(1)}, u32[]{:S(2)}) copy-start(f32[1280,512]{0,1:T(8,128)S(1)} %get-tuple-element.60) | copy-start | bytes 7864324
  170.9 25.6 %copy-start.11 = (f32[1280,512]{0,1:T(8,128)S(1)}, f32[1280,512]{0,1:T(8,128)}, u32[]{:S(2)}) copy-start(f32[1280,512]{0,1:T(8,128)} %get-tuple-element.126) | copy-start | bytes 7864324
  170.9 18.1 %collective-permute-start.24 = (bf16[1,128,512]{2,1,0:T(8,128)(2,1)S(1)}, bf16[1,128,512]{2,1,0:T(8,128)(2,1)S(1)}, u32[]{:S(2)}, u32[]{:S(2)}) collective-permute-start(bf16[1,128,512]{2,1,0:T(8,128)(2,1)S(1)} %get-tuple-element.92), channel_id=1, source_target_pairs={{0,8},{8,16},{16,24},{1,9},{9,17},{17,25},{2,10},{10,18},{18,26},{... | collective-permute-start | bytes 393224 | tf_op jit(solution)/shard_map/ppermute | solution.py:17
  178.8 17.6 %collective-permute-start.29 = (bf16[1,128,512]{2,1,0:T(8,128)(2,1)S(1)}, bf16[1,128,512]{2,1,0:T(8,128)(2,1)S(1)}, u32[]{:S(2)}, u32[]{:S(2)}) collective-permute-start(bf16[1,128,512]{2,1,0:T(8,128)(2,1)S(1)} %get-tuple-element.87), channel_id=1, source_target_pairs={{1,0},{3,2},{5,4},{7,6},{9,8},{11,10},{13,12},{15,14},{17,16},{19,... | collective-permute-start | bytes 393224 | tf_op jit(solution)/shard_map/ppermute | solution.py:18
  180.1 16.3 %collective-permute-start.28 = (bf16[1,128,512]{2,1,0:T(8,128)(2,1)S(1)}, bf16[1,128,512]{2,1,0:T(8,128)(2,1)S(1)}, u32[]{:S(2)}, u32[]{:S(2)}) collective-permute-start(bf16[1,128,512]{2,1,0:T(8,128)(2,1)S(1)} %get-tuple-element.88), channel_id=1, source_target_pairs={{0,1},{2,3},{4,5},{6,7},{8,9},{10,11},{12,13},{14,15},{16,17},{18,... | collective-permute-start | bytes 393224 | tf_op jit(solution)/shard_map/ppermute | solution.py:17
  184.7 11.7 %collective-permute-start.27 = (bf16[1,128,512]{2,1,0:T(8,128)(2,1)S(1)}, bf16[1,128,512]{2,1,0:T(8,128)(2,1)S(1)}, u32[]{:S(2)}, u32[]{:S(2)}) collective-permute-start(bf16[1,128,512]{2,1,0:T(8,128)(2,1)S(1)} %get-tuple-element.89), channel_id=1, source_target_pairs={{2,0},{4,2},{6,4},{3,1},{5,3},{7,5},{10,8},{12,10},{14,12},{11,9},... | collective-permute-start | bytes 393224 | tf_op jit(solution)/shard_map/ppermute | solution.py:18
  186.0 10.4 %collective-permute-start.26 = (bf16[1,128,512]{2,1,0:T(8,128)(2,1)S(1)}, bf16[1,128,512]{2,1,0:T(8,128)(2,1)S(1)}, u32[]{:S(2)}, u32[]{:S(2)}) collective-permute-start(bf16[1,128,512]{2,1,0:T(8,128)(2,1)S(1)} %get-tuple-element.90), channel_id=1, source_target_pairs={{0,2},{2,4},{4,6},{1,3},{3,5},{5,7},{8,10},{10,12},{12,14},{9,11},... | collective-permute-start | bytes 393224 | tf_op jit(solution)/shard_map/ppermute | solution.py:17
  189.0 7.3 %collective-permute-start.25 = (bf16[1,128,512]{2,1,0:T(8,128)(2,1)S(1)}, bf16[1,128,512]{2,1,0:T(8,128)(2,1)S(1)}, u32[]{:S(2)}, u32[]{:S(2)}) collective-permute-start(bf16[1,128,512]{2,1,0:T(8,128)(2,1)S(1)} %get-tuple-element.91), channel_id=1, source_target_pairs={{8,0},{16,8},{24,16},{9,1},{17,9},{25,17},{10,2},{18,10},{26,18},{... | collective-permute-start | bytes 393224 | tf_op jit(solution)/shard_map/ppermute | solution.py:18
  190.3 33.1 %slice-start.4 = ((s8[5242880]{0:T(1024)(128)(4,1)}), s8[4194304]{0:T(1024)(128)(4,1)S(1)}, s32[]{:S(2)}) async-start(s8[5242880]{0:T(1024)(128)(4,1)} %bitcast.310), calls=%async_computation.5 | async-start | bytes 8388608
  196.5 27.0 %slice-start.5 = ((s8[5242880]{0:T(1024)(128)(4,1)}), s8[1048576]{0:T(1024)(128)(4,1)S(1)}, s32[]{:S(2)}) async-start(s8[5242880]{0:T(1024)(128)(4,1)} %bitcast.310), calls=%async_computation.6 | async-start | bytes 2097152
  203.7 12.1 %collective-permute-start.30 = (bf16[1,128,512]{1,2,0:T(8,128)(2,1)S(1)}, bf16[1,128,512]{1,2,0:T(8,128)(2,1)S(1)}, u32[]{:S(2)}, u32[]{:S(2)}) collective-permute-start(bf16[1,128,512]{1,2,0:T(8,128)(2,1)S(1)} %get-tuple-element.86), channel_id=1, source_target_pairs={{0,8},{8,16},{16,24},{1,9},{9,17},{17,25},{2,10},{10,18},{18,26},{... | collective-permute-start | bytes 393224 | tf_op jit(solution)/shard_map/ppermute | solution.py:17
  205.6 17.7 %collective-permute-start.35 = (bf16[1,128,512]{1,2,0:T(8,128)(2,1)S(1)}, bf16[1,128,512]{1,2,0:T(8,128)(2,1)S(1)}, u32[]{:S(2)}, u32[]{:S(2)}) collective-permute-start(bf16[1,128,512]{1,2,0:T(8,128)(2,1)S(1)} %get-tuple-element.81), channel_id=1, source_target_pairs={{1,0},{3,2},{5,4},{7,6},{9,8},{11,10},{13,12},{15,14},{17,16},{19,... | collective-permute-start | bytes 393224 | tf_op jit(solution)/shard_map/ppermute | solution.py:18
  206.9 16.4 %collective-permute-start.34 = (bf16[1,128,512]{1,2,0:T(8,128)(2,1)S(1)}, bf16[1,128,512]{1,2,0:T(8,128)(2,1)S(1)}, u32[]{:S(2)}, u32[]{:S(2)}) collective-permute-start(bf16[1,128,512]{1,2,0:T(8,128)(2,1)S(1)} %get-tuple-element.82), channel_id=1, source_target_pairs={{0,1},{2,3},{4,5},{6,7},{8,9},{10,11},{12,13},{14,15},{16,17},{18,... | collective-permute-start | bytes 393224 | tf_op jit(solution)/shard_map/ppermute | solution.py:17
  211.5 11.8 %collective-permute-start.33 = (bf16[1,128,512]{1,2,0:T(8,128)(2,1)S(1)}, bf16[1,128,512]{1,2,0:T(8,128)(2,1)S(1)}, u32[]{:S(2)}, u32[]{:S(2)}) collective-permute-start(bf16[1,128,512]{1,2,0:T(8,128)(2,1)S(1)} %get-tuple-element.83), channel_id=1, source_target_pairs={{2,0},{4,2},{6,4},{3,1},{5,3},{7,5},{10,8},{12,10},{14,12},{11,9},... | collective-permute-start | bytes 393224 | tf_op jit(solution)/shard_map/ppermute | solution.py:18
  212.8 10.4 %collective-permute-start.32 = (bf16[1,128,512]{1,2,0:T(8,128)(2,1)S(1)}, bf16[1,128,512]{1,2,0:T(8,128)(2,1)S(1)}, u32[]{:S(2)}, u32[]{:S(2)}) collective-permute-start(bf16[1,128,512]{1,2,0:T(8,128)(2,1)S(1)} %get-tuple-element.84), channel_id=1, source_target_pairs={{0,2},{2,4},{4,6},{1,3},{3,5},{5,7},{8,10},{10,12},{12,14},{9,11},... | collective-permute-start | bytes 393224 | tf_op jit(solution)/shard_map/ppermute | solution.py:17
  215.9 7.3 %collective-permute-start.31 = (bf16[1,128,512]{1,2,0:T(8,128)(2,1)S(1)}, bf16[1,128,512]{1,2,0:T(8,128)(2,1)S(1)}, u32[]{:S(2)}, u32[]{:S(2)}) collective-permute-start(bf16[1,128,512]{1,2,0:T(8,128)(2,1)S(1)} %get-tuple-element.85), channel_id=1, source_target_pairs={{8,0},{16,8},{24,16},{9,1},{17,9},{25,17},{10,2},{18,10},{26,18},{... | collective-permute-start | bytes 393224 | tf_op jit(solution)/shard_map/ppermute | solution.py:18
  227.1 21.9 %copy-start.12 = (f32[1280,512]{0,1:T(8,128)S(1)}, f32[1280,512]{0,1:T(8,128)}, u32[]{:S(2)}) copy-start(f32[1280,512]{0,1:T(8,128)} %get-tuple-element.127) | copy-start | bytes 7864324
  227.1 14.1 %collective-permute-start.36 = (bf16[1,128,512]{2,1,0:T(8,128)(2,1)S(1)}, bf16[1,128,512]{2,1,0:T(8,128)(2,1)S(1)}, u32[]{:S(2)}, u32[]{:S(2)}) collective-permute-start(bf16[1,128,512]{2,1,0:T(8,128)(2,1)S(1)} %get-tuple-element.80), channel_id=1, source_target_pairs={{0,8},{8,16},{16,24},{1,9},{9,17},{17,25},{2,10},{10,18},{18,26},{... | collective-permute-start | bytes 393224 | tf_op jit(solution)/shard_map/ppermute | solution.py:17
  229.3 47.7 %slice-start.6 = ((s8[5242880]{0:T(1024)(128)(4,1)}), s8[4194304]{0:T(1024)(128)(4,1)S(1)}, s32[]{:S(2)}) async-start(s8[5242880]{0:T(1024)(128)(4,1)} %bitcast.313), calls=%async_computation.7 | async-start | bytes 8388608
  230.9 18.1 %collective-permute-start.41 = (bf16[1,128,512]{2,1,0:T(8,128)(2,1)S(1)}, bf16[1,128,512]{2,1,0:T(8,128)(2,1)S(1)}, u32[]{:S(2)}, u32[]{:S(2)}) collective-permute-start(bf16[1,128,512]{2,1,0:T(8,128)(2,1)S(1)} %get-tuple-element.75), channel_id=1, source_target_pairs={{1,0},{3,2},{5,4},{7,6},{9,8},{11,10},{13,12},{15,14},{17,16},{19,... | collective-permute-start | bytes 393224 | tf_op jit(solution)/shard_map/ppermute | solution.py:18
  232.3 16.6 %collective-permute-start.40 = (bf16[1,128,512]{2,1,0:T(8,128)(2,1)S(1)}, bf16[1,128,512]{2,1,0:T(8,128)(2,1)S(1)}, u32[]{:S(2)}, u32[]{:S(2)}) collective-permute-start(bf16[1,128,512]{2,1,0:T(8,128)(2,1)S(1)} %get-tuple-element.76), channel_id=1, source_target_pairs={{0,1},{2,3},{4,5},{6,7},{8,9},{10,11},{12,13},{14,15},{16,17},{18,... | collective-permute-start | bytes 393224 | tf_op jit(solution)/shard_map/ppermute | solution.py:17
  236.9 12.0 %collective-permute-start.39 = (bf16[1,128,512]{2,1,0:T(8,128)(2,1)S(1)}, bf16[1,128,512]{2,1,0:T(8,128)(2,1)S(1)}, u32[]{:S(2)}, u32[]{:S(2)}) collective-permute-start(bf16[1,128,512]{2,1,0:T(8,128)(2,1)S(1)} %get-tuple-element.77), channel_id=1, source_target_pairs={{2,0},{4,2},{6,4},{3,1},{5,3},{7,5},{10,8},{12,10},{14,12},{11,9},... | collective-permute-start | bytes 393224 | tf_op jit(solution)/shard_map/ppermute | solution.py:18
  238.2 10.7 %collective-permute-start.38 = (bf16[1,128,512]{2,1,0:T(8,128)(2,1)S(1)}, bf16[1,128,512]{2,1,0:T(8,128)(2,1)S(1)}, u32[]{:S(2)}, u32[]{:S(2)}) collective-permute-start(bf16[1,128,512]{2,1,0:T(8,128)(2,1)S(1)} %get-tuple-element.78), channel_id=1, source_target_pairs={{0,2},{2,4},{4,6},{1,3},{3,5},{5,7},{8,10},{10,12},{12,14},{9,11},... | collective-permute-start | bytes 393224 | tf_op jit(solution)/shard_map/ppermute | solution.py:17
  241.3 7.6 %collective-permute-start.37 = (bf16[1,128,512]{2,1,0:T(8,128)(2,1)S(1)}, bf16[1,128,512]{2,1,0:T(8,128)(2,1)S(1)}, u32[]{:S(2)}, u32[]{:S(2)}) collective-permute-start(bf16[1,128,512]{2,1,0:T(8,128)(2,1)S(1)} %get-tuple-element.79), channel_id=1, source_target_pairs={{8,0},{16,8},{24,16},{9,1},{17,9},{25,17},{10,2},{18,10},{26,18},{... | collective-permute-start | bytes 393224 | tf_op jit(solution)/shard_map/ppermute | solution.py:18
  249.0 28.0 %slice-start.7 = ((s8[5242880]{0:T(1024)(128)(4,1)}), s8[1048576]{0:T(1024)(128)(4,1)S(1)}, s32[]{:S(2)}) async-start(s8[5242880]{0:T(1024)(128)(4,1)} %bitcast.313), calls=%async_computation.8 | async-start | bytes 2097152
  254.8 13.7 %collective-permute-start.42 = (bf16[1,128,512]{1,2,0:T(8,128)(2,1)S(1)}, bf16[1,128,512]{1,2,0:T(8,128)(2,1)S(1)}, u32[]{:S(2)}, u32[]{:S(2)}) collective-permute-start(bf16[1,128,512]{1,2,0:T(8,128)(2,1)S(1)} %get-tuple-element.74), channel_id=1, source_target_pairs={{0,8},{8,16},{16,24},{1,9},{9,17},{17,25},{2,10},{10,18},{18,26},{... | collective-permute-start | bytes 393224 | tf_op jit(solution)/shard_map/ppermute | solution.py:17
  258.3 18.7 %collective-permute-start.47 = (bf16[1,128,512]{1,2,0:T(8,128)(2,1)S(1)}, bf16[1,128,512]{1,2,0:T(8,128)(2,1)S(1)}, u32[]{:S(2)}, u32[]{:S(2)}) collective-permute-start(bf16[1,128,512]{1,2,0:T(8,128)(2,1)S(1)} %get-tuple-element.69), channel_id=1, source_target_pairs={{1,0},{3,2},{5,4},{7,6},{9,8},{11,10},{13,12},{15,14},{17,16},{19,... | collective-permute-start | bytes 393224 | tf_op jit(solution)/shard_map/ppermute | solution.py:18
  259.6 17.3 %collective-permute-start.46 = (bf16[1,128,512]{1,2,0:T(8,128)(2,1)S(1)}, bf16[1,128,512]{1,2,0:T(8,128)(2,1)S(1)}, u32[]{:S(2)}, u32[]{:S(2)}) collective-permute-start(bf16[1,128,512]{1,2,0:T(8,128)(2,1)S(1)} %get-tuple-element.70), channel_id=1, source_target_pairs={{0,1},{2,3},{4,5},{6,7},{8,9},{10,11},{12,13},{14,15},{16,17},{18,... | collective-permute-start | bytes 393224 | tf_op jit(solution)/shard_map/ppermute | solution.py:17
  264.2 12.7 %collective-permute-start.45 = (bf16[1,128,512]{1,2,0:T(8,128)(2,1)S(1)}, bf16[1,128,512]{1,2,0:T(8,128)(2,1)S(1)}, u32[]{:S(2)}, u32[]{:S(2)}) collective-permute-start(bf16[1,128,512]{1,2,0:T(8,128)(2,1)S(1)} %get-tuple-element.71), channel_id=1, source_target_pairs={{2,0},{4,2},{6,4},{3,1},{5,3},{7,5},{10,8},{12,10},{14,12},{11,9},... | collective-permute-start | bytes 393224 | tf_op jit(solution)/shard_map/ppermute | solution.py:18
  265.5 11.3 %collective-permute-start.44 = (bf16[1,128,512]{1,2,0:T(8,128)(2,1)S(1)}, bf16[1,128,512]{1,2,0:T(8,128)(2,1)S(1)}, u32[]{:S(2)}, u32[]{:S(2)}) collective-permute-start(bf16[1,128,512]{1,2,0:T(8,128)(2,1)S(1)} %get-tuple-element.72), channel_id=1, source_target_pairs={{0,2},{2,4},{4,6},{1,3},{3,5},{5,7},{8,10},{10,12},{12,14},{9,11},... | collective-permute-start | bytes 393224 | tf_op jit(solution)/shard_map/ppermute | solution.py:17
  268.5 8.2 %collective-permute-start.43 = (bf16[1,128,512]{1,2,0:T(8,128)(2,1)S(1)}, bf16[1,128,512]{1,2,0:T(8,128)(2,1)S(1)}, u32[]{:S(2)}, u32[]{:S(2)}) collective-permute-start(bf16[1,128,512]{1,2,0:T(8,128)(2,1)S(1)} %get-tuple-element.73), channel_id=1, source_target_pairs={{8,0},{16,8},{24,16},{9,1},{17,9},{25,17},{10,2},{18,10},{26,18},{... | collective-permute-start | bytes 393224 | tf_op jit(solution)/shard_map/ppermute | solution.py:18
  285.2 7.2 %copy-start.1 = (bf16[1,1,1,1280,128]{4,3,2,1,0:T(8,128)(2,1)S(1)}, bf16[1,1,1,1280,128]{4,3,2,1,0:T(8,128)(2,1)}, u32[]{:S(2)}) copy-start(bf16[1,1,1,1280,128]{4,3,2,1,0:T(8,128)(2,1)} %param.18) | copy-start | bytes 983044
  (6 other events, 19.5 us)
Sparse Core Ops, SparseCore 0:
  10.4 37.1 all-reduce.1
where the time goes:
time: 301 us; the launch traced here: 299 us
  starting transfers between devices  119 us (40%)
  waiting for transfers between devices  85.5 us (28%)
  matrix products  38.2 us (13%)
  local copies, waits for them, and re-layouts  31.9 us (11%)
  between operations  19.3 us (6%)
  other arithmetic  5.15 us (2%)
    ppermute x24, starting transfers between devices, padded(): before = lax.ppermute(last, axis, up)  87.7 us
    ppermute x24, waiting for transfers between devices, padded(): after = lax.ppermute(leading, axis, down)  52.7 us
    psum x1, waiting for transfers between devices, body(): lax.psum(partial_value.astype(jnp.bfloat16), 'gx').astype(jnp.float32)  32.7 us
    ppermute x24, starting transfers between devices, padded(): after = lax.ppermute(leading, axis, down)  31.3 us
    dot_general x3, matrix products, body(): jnp.dot(kmat, extend_with(delta, lent_rows(delta, picks)), preferred_elem...  19.8 us
    unnamed x86, local copies, waits for them, and re-layouts  14.4 us
    dot_general x1, matrix products, body(): jnp.dot(kmat, extend_with(coarse_delta, lent_rows(coarse_delta, picks)),...  8.38 us
    another operation x8, local copies, waits for them, and re-layouts, lent_rows(): jnp.stack([lax.dynamic_slice_in_dim(field, picks[which] * BLK, BLK, 0) fo...  7.76 us
  transfers between devices with their start and end apart: 49, of which 9 were waited for; matrix products, arithmetic and copies ran while one was open for 4% of the time, Pallas kernels for 0%

commit v1 on v0

v1 whole, which is shorter than its diff:
```python
import functools

import jax
import jax.numpy as jnp
from jax import lax
from jax.experimental import pallas as pl
from jax.experimental.pallas import tpu as pltpu
from jax.sharding import PartitionSpec as P

BLK = 128
NCOLOR = 4
TM = 256
HALVES = 2
MESH = pl.DeviceIdType.MESH
BF = jnp.bfloat16
F32 = jnp.float32
AXES = ("gx", "gx", "gy", "gy", "col", "col")


def flat(x):
    return x.reshape(-1, x.shape[-1])


def dot(a, b):
    return jnp.dot(a, b, preferred_element_type=F32)


def kernel(sizes, colors, lend, rhs, stiff, inv, basis, emat, out,
           kmat, ainv, phi, ecoarse, resid, resid_b, y, delta, acc, out_b,
           margin, lent, k_lent, e_lent, weights, sols, base_m, base_l,
           part, line_in, line_out,
           load_sem, store_sem, send_sem, recv_sem, sol_send, sol_recv,
           base_send, base_recv, line_send, line_recv):
    own = ainv.shape[0]
    ncg = phi.shape[2]
    width = resid.shape[3]
    at = {axis: lax.axis_index(axis) for axis in sizes}

    def has(side):
        i = at[AXES[side]]
        return i > 0 if side % 2 == 0 else i < sizes[AXES[side]] - 1

    def peer(side):
        i = at[AXES[side]]
        return {AXES[side]: i - 1 if side % 2 == 0 else i + 1}

    loads = [pltpu.make_async_copy(basis.at[0, 0, 0], phi, load_sem.at[0])]
    for h in range(HALVES):
        loads.append(pltpu.make_async_copy(
            rhs.at[0, 0, 0, :, :, h * width:(h + 1) * width], resid.at[h], load_sem.at[1 + h]))
    loads.append(pltpu.make_async_copy(emat.at[0, 0], ecoarse, load_sem.at[3]))
    loads.append(pltpu.make_async_copy(stiff.at[0, 0, 0], kmat, load_sem.at[4]))
    loads.append(pltpu.make_async_copy(inv.at[0, 0, 0], ainv, load_sem.at[5]))
    for load in loads:
        load.start()

    barrier = pltpu.get_barrier_semaphore()
    for side in range(6):
        @pl.when(has(side))
        def _(side=side):
            pl.semaphore_signal(barrier, inc=1, device_id=peer(side), device_id_type=MESH)

    for side in range(6):
        @pl.when(jnp.logical_not(has(side)))
        def _(side=side):
            rows = pl.ds(side * BLK, BLK)
            base_m[rows, :] = jnp.zeros((BLK, ncg), BF)
            for r in range(2 * NCOLOR - 1):
                for h in range(HALVES):
                    margin[r, h, rows, :] = jnp.zeros((BLK, width), BF)
            if side >= 2:
                for h in range(HALVES):
                    sols[h, pl.ds((side - 1) * ncg, ncg), :] = jnp.zeros((ncg, width), BF)
            else:
                for h in range(HALVES):
                    line_in[side, h] = jnp.zeros((ncg, width), BF)

    picks = [lend[0, 0, 0, side] for side in range(6)]
    color = colors[0, 0, 0]

    pl.semaphore_wait(barrier, sum(has(side).astype(jnp.int32) for side in range(6)))

    def margin_copy(r, h, side):
        return pltpu.make_async_remote_copy(
            src_ref=lent.at[r, h, pl.ds(side * BLK, BLK)],
            dst_ref=margin.at[r, h, pl.ds((side ^ 1) * BLK, BLK)],
            send_sem=send_sem.at[r, h, side], recv_sem=recv_sem.at[r, h, side ^ 1],
            device_id=peer(side), device_id_type=MESH)

    def margin_arrival(r, h, side):
        return pltpu.make_async_remote_copy(
            src_ref=lent.at[r, h, pl.ds(side * BLK, BLK)],
            dst_ref=margin.at[r, h, pl.ds(side * BLK, BLK)],
            send_sem=send_sem.at[r, h, side], recv_sem=recv_sem.at[r, h, side],
            device_id=peer(side), device_id_type=MESH)

    def base_copy(side, slot):
        return pltpu.make_async_remote_copy(
            src_ref=base_l.at[pl.ds(side * BLK, BLK)],
            dst_ref=base_m.at[pl.ds(slot * BLK, BLK)],
            send_sem=base_send.at[side], recv_sem=base_recv.at[slot],
            device_id=peer(side), device_id_type=MESH)

    def sol_copy(h, side, slot):
        return pltpu.make_async_remote_copy(
            src_ref=sols.at[h, pl.ds(0, ncg)],
            dst_ref=sols.at[h, pl.ds((slot - 1) * ncg, ncg)],
            send_sem=sol_send.at[h, side], recv_sem=sol_recv.at[h, slot],
            device_id=peer(side), device_id_type=MESH)

    def line_copy(h, side, slot):
        return pltpu.make_async_remote_copy(
            src_ref=line_out.at[side, h], dst_ref=line_in.at[slot, h],
            send_sem=line_send.at[side, h], recv_sem=line_recv.at[slot, h],
            device_id=peer(side), device_id_type=MESH)

    def each(sides, make, action):
        for side in sides:
            @pl.when(has(side))
            def _(side=side):
                getattr(make(side), action)()

    def send_margins(r, h):
        each(range(6), functools.partial(margin_copy, r, h), "start")

    def await_margins(r, h):
        each(range(6), functools.partial(margin_arrival, r, h), "wait_recv")

    def tiles(body, rows=own):
        def step(i, carry):
            body(pl.ds(pl.multiple_of(i * TM, TM), TM), pl.ds(i * (TM // BLK), TM // BLK))
            return carry
        lax.fori_loop(0, rows // TM, step, 0)

    loads[0].wait()
    for side in range(6):
        base_l[pl.ds(side * BLK, BLK), :] = phi[picks[side]]
    each(range(6), lambda side: base_copy(side, side ^ 1), "start")
    phi_t = phi[...].reshape(own, ncg).T
    for h in range(HALVES):
        loads[1 + h].wait()
        part[h] = dot(phi_t, resid[h].reshape(own, width).astype(BF))

    n_line = sizes["gx"]
    low = at["gx"] < n_line // 2

    def pass_on(h, slot):
        @pl.when(has(slot))
        def _():
            line_copy(h, slot, slot).wait_recv()

        @pl.when(has(slot ^ 1))
        def _():
            line_out[slot ^ 1, h] = (line_in[slot, h].astype(F32) + part[h]).astype(BF)
            line_copy(h, slot ^ 1, slot).start()

    def pass_all(slot):
        for h in range(HALVES):
            pass_on(h, slot)

    pl.when(low)(lambda: pass_all(0))
    pl.when(jnp.logical_not(low))(lambda: pass_all(1))

    loads[4].wait()
    for side in range(6):
        k_lent[pl.ds(side * BLK, BLK), :] = kmat[picks[side], :, 0:own]
    each(range(6), lambda side: base_copy(side, side), "wait_recv")

    def weigh(rows, blocks):
        first = dot(flat(kmat[blocks, :, 0:own]), phi[...].reshape(own, ncg))
        first = first + dot(flat(kmat[blocks, :, own:own + 2 * BLK]), base_m[0:2 * BLK, :])
        weights[rows, 0:ncg] = first.astype(BF)
        for side in range(2, 6):
            weights[rows, (side - 1) * ncg:side * ncg] = dot(
                flat(kmat[blocks, :, own + side * BLK:own + (side + 1) * BLK]),
                base_m[side * BLK:(side + 1) * BLK, :]).astype(BF)

    tiles(weigh)

    pl.when(low)(lambda: pass_all(1))
    pl.when(jnp.logical_not(low))(lambda: pass_all(0))

    loads[3].wait()
    for h in range(HALVES):
        total = line_in[0, h].astype(F32) + part[h] + line_in[1, h].astype(F32)
        sols[h, 0:ncg, :] = jnp.dot(
            ecoarse[...], total, precision=lax.Precision.HIGHEST,
            preferred_element_type=F32).astype(BF)
        each(range(2, 6), lambda side, h=h: sol_copy(h, side, side ^ 1), "start")
    for h in range(HALVES):
        def coarse(rows, blocks, h=h):
            acc[h, rows, :] = dot(flat(phi[blocks]), sols[h, 0:ncg, :])
        tiles(coarse)

    def lend_resid(r, h, with_own):
        for side in range(6):
            block = pl.ds(side * BLK, BLK)
            value = resid[h, picks[side]]
            if with_own:
                value = value - e_lent[h, block, :]
            lent[r, h, block, :] = value.astype(BF)
        send_margins(r, h)

    for h in range(HALVES):
        each(range(2, 6), lambda side, h=h: sol_copy(h, side, side), "wait_recv")

        def first_resid(rows, blocks, h=h):
            value = flat(resid[h, blocks]) - dot(weights[rows, :], sols[h])
            resid[h, blocks] = value.reshape(-1, BLK, width)
            resid_b[h, rows, :] = value.astype(BF)
        tiles(first_resid)
        lend_resid(0, h, False)

    loads[5].wait()

    def solve_own(h):
        def body(rows, blocks):
            y[h, rows, :] = dot(ainv[rows, 0:own], resid_b[h])
        tiles(body)

    for h in range(HALVES):
        solve_own(h)

    for c in range(NCOLOR):
        mine = (color == c).astype(F32)
        last = c == NCOLOR - 1
        for h in range(HALVES):
            await_margins(2 * c, h)

            def solve(rows, blocks, h=h):
                value = (y[h, rows, :] + dot(ainv[rows, own:], margin[2 * c, h])) * mine
                if last:
                    out_b[h, rows, :] = (acc[h, rows, :] + value).astype(BF)
                else:
                    delta[h, blocks] = value.astype(BF).reshape(-1, BLK, width)
                    acc[h, rows, :] += value
            tiles(solve)
            if last:
                pltpu.make_async_copy(
                    out_b.at[h], out.at[0, 0, 0, :, h * width:(h + 1) * width],
                    store_sem.at[h]).start()
            else:
                for side in range(6):
                    lent[2 * c + 1, h, pl.ds(side * BLK, BLK), :] = delta[h, picks[side]]
                send_margins(2 * c + 1, h)
        if last:
            break
        for h in range(HALVES):
            def own_part(rows, blocks, h=h):
                value = dot(k_lent[rows, :], delta[h].reshape(own, width))
                if c == 0:
                    e_lent[h, rows, :] = value
                else:
                    e_lent[h, rows, :] += value
            tiles(own_part, 6 * BLK)
        for h in range(HALVES):
            await_margins(2 * c + 1, h)

            def update(rows, blocks, h=h):
                value = flat(resid[h, blocks]) - dot(flat(kmat[blocks, :, own:]), margin[2 * c + 1, h])
                resid[h, blocks] = value.reshape(-1, BLK, width)
                resid_b[h, rows, :] = value.astype(BF)
            tiles(update)
            lend_resid(2 * c + 2, h, True)
        for h in range(HALVES):
            solve_own(h)

    for h in range(HALVES):
        pltpu.make_async_copy(
            out_b.at[h], out.at[0, 0, 0, :, h * width:(h + 1) * width], store_sem.at[h]).wait()
    each(range(6), lambda side: base_copy(side, side ^ 1), "wait_send")
    for h in range(HALVES):
        each(range(2), lambda side, h=h: line_copy(h, side, side ^ 1), "wait_send")
        each(range(2, 6), lambda side, h=h: sol_copy(h, side, side ^ 1), "wait_send")
        for r in range(2 * NCOLOR - 1):
            each(range(6), functools.partial(margin_copy, r, h), "wait_send")


def in_blocks(x):
    return x.reshape(x.shape[:-2] + (x.shape[-2] // BLK, BLK, x.shape[-1]))


def body(sizes, rhs, stiff, inv_local, basis, coarse_inv, colors, lend):
    own, nrhs = rhs.shape[-2:]
    sub = stiff.shape[-1]
    ncg = basis.shape[-1]
    width = nrhs // HALVES
    count = own // BLK
    rounds = 2 * NCOLOR - 1
    edge = 6 * BLK
    dma = pltpu.SemaphoreType.DMA
    smem = pl.BlockSpec(memory_space=pltpu.SMEM)
    anyw = pl.BlockSpec(memory_space=pl.ANY)
    result = pl.pallas_call(
        functools.partial(kernel, sizes),
        out_shape=jax.ShapeDtypeStruct(rhs.shape, BF),
        in_specs=[smem, smem] + [anyw] * 5,
        out_specs=anyw,
        scratch_shapes=[
            pltpu.VMEM((count, BLK, sub), BF),
            pltpu.VMEM((own, sub), BF),
            pltpu.VMEM((count, BLK, ncg), BF),
            pltpu.VMEM((ncg, ncg), F32),
            pltpu.VMEM((HALVES, count, BLK, width), F32),
            pltpu.VMEM((HALVES, own, width), BF),
            pltpu.VMEM((HALVES, own, width), F32),
            pltpu.VMEM((HALVES, count, BLK, width), BF),
            pltpu.VMEM((HALVES, own, width), F32),
            pltpu.VMEM((HALVES, own, width), BF),
            pltpu.VMEM((rounds, HALVES, edge, width), BF),
            pltpu.VMEM((rounds, HALVES, edge, width), BF),
            pltpu.VMEM((edge, own), BF),
            pltpu.VMEM((HALVES, edge, width), F32),
            pltpu.VMEM((own, 5 * ncg), BF),
            pltpu.VMEM((HALVES, 5 * ncg, width), BF),
            pltpu.VMEM((edge, ncg), BF),
            pltpu.VMEM((edge, ncg), BF),
            pltpu.VMEM((HALVES, ncg, width), F32),
            pltpu.VMEM((2, HALVES, ncg, width), BF),
            pltpu.VMEM((2, HALVES, ncg, width), BF),
            dma((6,)),
            dma((HALVES,)),
            dma((rounds, HALVES, 6)),
            dma((rounds, HALVES, 6)),
            dma((HALVES, 6)),
            dma((HALVES, 6)),
            dma((6,)),
            dma((6,)),
            dma((2, HALVES)),
            dma((2, HALVES)),
        ],
        compiler_params=pltpu.CompilerParams(
            collective_id=0, has_side_effects=True, vmem_limit_bytes=58 * 2**20),
    )(colors, lend, in_blocks(rhs), in_blocks(stiff), inv_local, in_blocks(basis), coarse_inv)
    return result.astype(F32)


def solution(mesh):
    in_specs = (
        P("gx", "gy", "col", None, None),
        P("gx", "gy", "col", None, None),
        P("gx", "gy", "col", None, None),
        P("gx", "gy", "col", None, None),
        P("gy", "col", None, None),
        P("gx", "gy", "col"),
        P("gx", "gy", "col", None),
    )
    out_specs = P("gx", "gy", "col", None, None)
    return jax.shard_map(functools.partial(body, dict(mesh.shape)), mesh=mesh,
                         in_specs=in_specs, out_specs=out_specs, check_vma=False)
```

time: 301 us -> 73 us (0.24)
  starting transfers between devices: 119 us -> 0 us
  waiting for transfers between devices: 85.5 us -> 0 us
  Pallas kernels: 0 us -> 69 us
  matrix products: 38.2 us -> 0 us
  local copies, waits for them, and re-layouts: 31.9 us -> 0 us
  between operations: 19.3 us -> 0.66 us
    ppermute x48 -> x0, starting transfers between devices: 119 us -> none  [the longest x24 87.7 us: padded(): before = lax.ppermute(last, axis, up)]
    pallas_call x0 -> x1, Pallas kernels: none -> 69 us  [body(): pl.pallas_call(functools.partial(kernel, sizes), out_shape=jax.ShapeDtype...]
    ppermute x48 -> x0, waiting for transfers between devices: 52.7 us -> none  [the longest x24 52.7 us: padded(): after = lax.ppermute(leading, axis, down)]
    dot_general x8 -> x0, matrix products: 38.2 us -> none  [the longest x3 19.8 us: body(): jnp.dot(kmat, extend_with(delta, lent_rows(delta, picks)), preferred_elem...]
    psum x1 -> x0, waiting for transfers between devices: 32.7 us -> none  [body(): lax.psum(partial_value.astype(jnp.bfloat16), 'gx').astype(jnp.float32)]
    unnamed x86 -> x0, local copies, waits for them, and re-layouts: 14.4 us -> none
    another operation x14 -> x0, local copies, waits for them, and re-layouts: 11.7 us -> none  [the longest x8 7.76 us: lent_rows(): jnp.stack([lax.dynamic_slice_in_dim(field, picks[which] * BLK, BLK, 0) fo...]
    broadcast_in_dim x1 -> x0, other arithmetic: 5.15 us -> none  [body(): return acc[None, None, None]]
  transfers between devices with their start and end apart: 49 -> 0, of which waited for: 9 -> 0; matrix products, arithmetic and copies ran while one was open for 4% -> 0% of each run, Pallas kernels for 0% -> 0%
where the time goes in v1:
time: 73 us; the launch traced here: 72.9 us
  Pallas kernels  69 us (95%)
  other arithmetic  3.18 us (4%)
    pallas_call x1, Pallas kernels, body(): pl.pallas_call(functools.partial(kernel, sizes), out_shape=jax.ShapeDtype...  69 us
    convert_element_type x1, other arithmetic, body(): return result.astype(F32)  3.18 us

profile of v1, /device:TPU:0, one launch (start us, length us, event | category | flops | bytes accessed | tf_op | source)
XLA Modules:
  0.0 72.9 jit_solution(7507028220414629970)
XLA Ops:
  0.7 69.0 %shard_map.73 = bf16[1,1,1,1280,512]{4,3,2,1,0:T(8,128)(2,1)} custom-call(s32[1,1,1]{2,1,0:T(1,128)S(6)} %copy.8.colors, s32[1,1,1,6]{3,2,1,0:T(1,128)} %lend.1, f32[1,1,1,10,128,512]{5,4,3,2,1,0:T(8,128)} %bitcast.4, bf16[1,1,1,10,128,2048]{5,4,3,2,1,0:T(8,128)(2,1)} %bitcast.3, bf16[1,1,1,1280,2048]{4,3,2,1,0:T(8,128)(2,1)} %inv.1, ...), custom_call_target="tpu_custom_call" | custom-call | tf_op jit(solution)/shard_map/pallas_call | solution.py:294
  69.7 3.2 %convert_element_type.3 = f32[1,1,1,1280,512]{4,3,2,1,0:T(8,128)} convert(bf16[1,1,1,1280,512]{4,3,2,1,0:T(8,128)(2,1)} %shard_map.73) | non-fusion elementwise | flops 655360 | bytes 3932160 | tf_op jit(solution)/shard_map/convert_element_type | solution.py:335

commit v2 on v1

--- a/solution.py
+++ b/solution.py
@@ -9,7 +9,8 @@
 
 BLK = 128
 NCOLOR = 4
-TM = 256
+TM = 640
+TE = 768
 HALVES = 2
 MESH = pl.DeviceIdType.MESH
 BF = jnp.bfloat16
@@ -127,10 +128,12 @@
         each(range(6), functools.partial(margin_arrival, r, h), "wait_recv")
 
     def tiles(body, rows=own):
+        tm = TM if rows == own else TE
+
         def step(i, carry):
-            body(pl.ds(pl.multiple_of(i * TM, TM), TM), pl.ds(i * (TM // BLK), TM // BLK))
+            body(pl.ds(pl.multiple_of(i * tm, tm), tm), pl.ds(i * (tm // BLK), tm // BLK))
             return carry
-        lax.fori_loop(0, rows // TM, step, 0)
+        lax.fori_loop(0, rows // tm, step, 0)
 
     loads[0].wait()
     for side in range(6):

time: 73 us -> 62.7 us (0.86)
  Pallas kernels: 69 us -> 58.7 us
    pallas_call x1, Pallas kernels: 69 us -> 58.7 us  [body(): pl.pallas_call(functools.partial(kernel, sizes), out_shape=jax.ShapeDtype...]
where the time goes in v2:
time: 62.7 us; the launch traced here: 62.5 us
  Pallas kernels  58.7 us (94%)
  other arithmetic  3.18 us (5%)
  between operations  0.66 us (1%)
    pallas_call x1, Pallas kernels, body(): pl.pallas_call(functools.partial(kernel, sizes), out_shape=jax.ShapeDtype...  58.7 us
    convert_element_type x1, other arithmetic, body(): return result.astype(F32)  3.18 us

profile of v2, /device:TPU:0, one launch (start us, length us, event | category | flops | bytes accessed | tf_op | source)
XLA Modules:
  0.0 62.5 jit_solution(16555998179166460874)
XLA Ops:
  0.7 58.7 %shard_map.73 = bf16[1,1,1,1280,512]{4,3,2,1,0:T(8,128)(2,1)} custom-call(s32[1,1,1]{2,1,0:T(1,128)S(6)} %copy.8.colors, s32[1,1,1,6]{3,2,1,0:T(1,128)} %lend.1, f32[1,1,1,10,128,512]{5,4,3,2,1,0:T(8,128)} %bitcast.4, bf16[1,1,1,10,128,2048]{5,4,3,2,1,0:T(8,128)(2,1)} %bitcast.3, bf16[1,1,1,1280,2048]{4,3,2,1,0:T(8,128)(2,1)} %inv.1, ...), custom_call_target="tpu_custom_call" | custom-call | tf_op jit(solution)/shard_map/pallas_call | solution.py:297
  59.4 3.2 %convert_element_type.3 = f32[1,1,1,1280,512]{4,3,2,1,0:T(8,128)} convert(bf16[1,1,1,1280,512]{4,3,2,1,0:T(8,128)(2,1)} %shard_map.73) | non-fusion elementwise | flops 655360 | bytes 3932160 | tf_op jit(solution)/shard_map/convert_element_type | solution.py:338

commit v3 on v2

--- a/solution.py
+++ b/solution.py
@@ -52,7 +52,7 @@
     loads.append(pltpu.make_async_copy(emat.at[0, 0], ecoarse, load_sem.at[3]))
     loads.append(pltpu.make_async_copy(stiff.at[0, 0, 0], kmat, load_sem.at[4]))
     loads.append(pltpu.make_async_copy(inv.at[0, 0, 0], ainv, load_sem.at[5]))
-    for load in loads:
+    for load in loads[:4]:
         load.start()
 
     barrier = pltpu.get_barrier_semaphore()
@@ -142,6 +142,8 @@
     phi_t = phi[...].reshape(own, ncg).T
     for h in range(HALVES):
         loads[1 + h].wait()
+        if h == HALVES - 1:
+            loads[4].start()
         part[h] = dot(phi_t, resid[h].reshape(own, width).astype(BF))
 
     n_line = sizes["gx"]
@@ -165,6 +167,7 @@
     pl.when(jnp.logical_not(low))(lambda: pass_all(1))
 
     loads[4].wait()
+    loads[5].start()
     for side in range(6):
         k_lent[pl.ds(side * BLK, BLK), :] = kmat[picks[side], :, 0:own]
     each(range(6), lambda side: base_copy(side, side), "wait_recv")
@@ -233,10 +236,11 @@
             def solve(rows, blocks, h=h):
                 value = (y[h, rows, :] + dot(ainv[rows, own:], margin[2 * c, h])) * mine
                 if last:
+                    for before in range(c):
+                        value = value + flat(delta[before, h, blocks]).astype(F32)
                     out_b[h, rows, :] = (acc[h, rows, :] + value).astype(BF)
                 else:
-                    delta[h, blocks] = value.astype(BF).reshape(-1, BLK, width)
-                    acc[h, rows, :] += value
+                    delta[c, h, blocks] = value.astype(BF).reshape(-1, BLK, width)
             tiles(solve)
             if last:
                 pltpu.make_async_copy(
@@ -244,13 +248,13 @@
                     store_sem.at[h]).start()
             else:
                 for side in range(6):
-                    lent[2 * c + 1, h, pl.ds(side * BLK, BLK), :] = delta[h, picks[side]]
+                    lent[2 * c + 1, h, pl.ds(side * BLK, BLK), :] = delta[c, h, picks[side]]
                 send_margins(2 * c + 1, h)
         if last:
             break
         for h in range(HALVES):
             def own_part(rows, blocks, h=h):
-                value = dot(k_lent[rows, :], delta[h].reshape(own, width))
+                value = dot(k_lent[rows, :], delta[c, h].reshape(own, width))
                 if c == 0:
                     e_lent[h, rows, :] = value
                 else:
@@ -307,7 +311,7 @@
             pltpu.VMEM((HALVES, count, BLK, width), F32),
             pltpu.VMEM((HALVES, own, width), BF),
             pltpu.VMEM((HALVES, own, width), F32),
-            pltpu.VMEM((HALVES, count, BLK, width), BF),
+            pltpu.VMEM((NCOLOR - 1, HALVES, count, BLK, width), BF),
             pltpu.VMEM((HALVES, own, width), F32),
             pltpu.VMEM((HALVES, own, width), BF),
             pltpu.VMEM((rounds, HALVES, edge, width), BF),

time: 62.7 us -> 63.1 us (level)
  no operation moved by 1% of the time
where the time goes in v3:
time: 63.1 us; the launch traced here: 62.9 us
  Pallas kernels  59 us (94%)
  other arithmetic  3.18 us (5%)
  between operations  0.66 us (1%)
    pallas_call x1, Pallas kernels, body(): pl.pallas_call(functools.partial(kernel, sizes), out_shape=jax.ShapeDtype...  59 us
    convert_element_type x1, other arithmetic, body(): return result.astype(F32)  3.18 us

profile of v3, /device:TPU:0, one launch (start us, length us, event | category | flops | bytes accessed | tf_op | source)
XLA Modules:
  0.0 62.9 jit_solution(13759217700084342373)
XLA Ops:
  0.7 59.0 %shard_map.73 = bf16[1,1,1,1280,512]{4,3,2,1,0:T(8,128)(2,1)} custom-call(s32[1,1,1]{2,1,0:T(1,128)S(6)} %copy.8.colors, s32[1,1,1,6]{3,2,1,0:T(1,128)} %lend.1, f32[1,1,1,10,128,512]{5,4,3,2,1,0:T(8,128)} %bitcast.4, bf16[1,1,1,10,128,2048]{5,4,3,2,1,0:T(8,128)(2,1)} %bitcast.3, bf16[1,1,1,1280,2048]{4,3,2,1,0:T(8,128)(2,1)} %inv.1, ...), custom_call_target="tpu_custom_call" | custom-call | tf_op jit(solution)/shard_map/pallas_call | solution.py:301
  59.7 3.2 %convert_element_type.3 = f32[1,1,1,1280,512]{4,3,2,1,0:T(8,128)} convert(bf16[1,1,1,1280,512]{4,3,2,1,0:T(8,128)(2,1)} %shard_map.73) | non-fusion elementwise | flops 655360 | bytes 3932160 | tf_op jit(solution)/shard_map/convert_element_type | solution.py:342
